TPU v7x, 32 devices: a whole 2x2x4 slice. The times are simulated.
32 devices in a mesh: scalp: 16 (over z, y, x), screen: 2 (over core).
Axes of the slice: x: 2, y: 2, z: 4, core: 2. Of those that a mesh axis runs over, the one named last changes fastest.
Arguments:
- guides: bfloat16 [65536, 384], P('scalp'), may hold values from -6 to 6
- neighbours: int32 [128, 32], P(('scalp', 'screen')), may hold values from 0 to 65535, as said below
- pick: int32 [128, 4, 256], P(('scalp', 'screen')), may hold values from 0 to 31, as said below
- pick_weight: bfloat16 [128, 4, 256], P(('scalp', 'screen')), may hold values from 0.099609375 to 0.59765625
- keep: int32 [128, 256], P(('scalp', 'screen')), may hold values 0 or 1
- width: float32 [128, 256], P(('scalp', 'screen')), may hold values from 0.2 to 2
- route: int32 [128, 1], P(('scalp', 'screen')), may hold values from 0 to 1; in each aligned block of 4 rows (0 to 3, 4 to 7, ...) at most 3 rows name the same one
- tess_centre: bfloat16 [2, 384, 768], P('screen'), may hold values from -0.3125 to 0.3125
- tess_side: bfloat16 [2, 384, 768], P('screen'), may hold values from -0.3125 to 0.3125
Outputs:
- ribbon: bfloat16 [49152, 768], P(('scalp', 'screen'))
Inputs may be any that keep to these rules, and one draw needn't show every extreme that they name: `neighbours`: each entry names a guide of the render block's own scalp tile or of the scalp tile just before or after it, wrapping around; a block of device (s, c) belongs to scalp tile s. `pick`: the 4 entries of one render strand differ. `route`: among the 4 blocks of one device at most 3 name the same screen tile.
All inputs are finite; a program needn't handle non-finite values. No bound on the sum of `keep` on one device may be relied on, other than what follows from the above.
Results may differ from a plain program's by a relative error of at most 0.009.
Values may be sent and summed in bfloat16 or wider, within the bound.
A program may use at most 64 MiB of HBM per device.

v0:
```python
import jax
import jax.numpy as jnp
from jax import lax
from jax.sharding import PartitionSpec as P


def extended(block, sides, width):
    for axis, dim in sides:
        count = lax.axis_size(axis)
        forward = [(i, i + 1) for i in range(count - 1)]
        forward.append((count - 1, 0))
        backward = [(target, source) for source, target in forward]
        low = lax.ppermute(
            lax.slice_in_dim(block, block.shape[dim] - width, None, axis=dim), axis, forward
        )
        high = lax.ppermute(lax.slice_in_dim(block, 0, width, axis=dim), axis, backward)
        block = jnp.concatenate([low, block, high], axis=dim)
    return block


def shifted(x, axis, by):
    devices = lax.axis_size(axis)
    return lax.ppermute(x, axis, [(i, (i + by) % devices) for i in range(devices)])


def blend(picks, weights, count):
    hit = (picks[..., None] == jnp.arange(count, dtype=jnp.int32)).astype(jnp.float32)
    return jnp.sum(hit * weights.astype(jnp.float32)[..., None], axis=1).astype(jnp.bfloat16)


def shards(guides, neighbours, pick, pick_weight, keep, width, route, tess_centre, tess_side):
    scalps = lax.axis_size("scalp")
    screens = lax.axis_size("screen")
    tile = guides.shape[0]
    blocks = neighbours.shape[0]
    listed = neighbours.shape[1]
    strands = keep.shape[1]
    slots_each = blocks // screens + blocks // 4
    centre_map = tess_centre[0]
    side_map = tess_side[0]
    here = lax.axis_index("scalp")
    owner = neighbours // tile
    relative = jnp.mod(owner - here + 1, scalps)
    lists = extended(neighbours, (("scalp", 0),), blocks)
    lower_list = lists[:blocks]
    upper_list = lists[2 * blocks :]
    for_lower = guides[lower_list % tile]
    for_upper = guides[upper_list % tile]
    from_upper = shifted(for_lower, "scalp", -1)
    from_lower = shifted(for_upper, "scalp", 1)
    own_rows = guides[neighbours % tile]
    gathered = jnp.where(
        (relative == 1)[..., None],
        own_rows,
        jnp.where((relative == 0)[..., None], from_lower, from_upper),
    )
    mixing = blend(pick, pick_weight, listed)
    kept = keep.astype(jnp.float32)
    scaled = width * strands / (jnp.sum(kept, axis=1, keepdims=True) + 1.0)
    tiles = route[:, 0]
    same = tiles[:, None] == tiles[None, :]
    earlier = jnp.arange(blocks)[None, :] < jnp.arange(blocks)[:, None]
    rank = jnp.sum(same & earlier, axis=1)
    slot = tiles * slots_each + rank
    select = slot[None, :] == jnp.arange(screens * slots_each, dtype=jnp.int32)[:, None]
    select_half = select.astype(jnp.bfloat16)
    select_full = select.astype(jnp.float32)
    kept_packed = jnp.dot(select_full, kept, precision=lax.Precision.HIGHEST).reshape(
        screens, slots_each, strands
    )
    scaled_packed = jnp.dot(select_full, scaled, precision=lax.Precision.HIGHEST).reshape(
        screens, slots_each, strands
    )
    panel = jnp.einsum("rbk,rkx->rbx", mixing, gathered, preferred_element_type=jnp.float32).astype(
        jnp.bfloat16
    )
    panel_packed = jnp.einsum(
        "sr,rbx->sbx", select_half, panel, preferred_element_type=jnp.float32
    ).astype(jnp.bfloat16)
    panel_packed = panel_packed.reshape(screens, slots_each, strands, panel.shape[2])
    panel = lax.all_to_all(panel_packed, "screen", split_axis=0, concat_axis=0, tiled=True)
    flat = panel.reshape(-1, panel.shape[-1])
    centre = jnp.dot(flat, centre_map, preferred_element_type=jnp.float32)
    side = jnp.dot(flat, side_map, preferred_element_type=jnp.float32)
    vertex = lax.all_to_all(
        kept_packed.astype(jnp.bfloat16), "screen", split_axis=0, concat_axis=0, tiled=True
    ).astype(kept_packed.dtype).reshape(-1, 1) * (
        centre
        + lax.all_to_all(
            scaled_packed.astype(jnp.bfloat16), "screen", split_axis=0, concat_axis=0, tiled=True
        )
        .astype(scaled_packed.dtype)
        .reshape(-1, 1)
        * side
    )
    received = vertex.astype(jnp.bfloat16).reshape(panel.shape[:3] + (centre.shape[1],))
    return received.reshape(-1, received.shape[-1])


def solution(mesh):
    return jax.shard_map(
        shards,
        mesh=mesh,
        in_specs=(
            P("scalp", None),
            P(("scalp", "screen"), None),
            P(("scalp", "screen"), None, None),
            P(("scalp", "screen"), None, None),
            P(("scalp", "screen"), None),
            P(("scalp", "screen"), None),
            P(("scalp", "screen"), None),
            P("screen", None, None),
            P("screen", None, None),
        ),
        out_specs=P(("scalp", "screen"), None),
        check_vma=False,
    )
```

profile of v0, /device:TPU:0, one launch (start us, length us, event | category | flops | bytes accessed | tf_op | source)
XLA Modules:
  0.0 45.9 jit_solution(8918014541948590514)
XLA Ops:
  0.0 0.0 copy-start
  0.0 2.9 %collective-permute-start.2 = (s32[4,32]{1,0:T(4,128)}, s32[4,32]{1,0:T(4,128)S(1)}, u32[]{:S(2)}, u32[]{:S(2)}) collective-permute-start(s32[4,32]{1,0:T(4,128)} %param.10), channel_id=1, source_target_pairs={{0,2},{2,4},{4,6},{6,8},{8,10},{10,12},{12,14},{14,16},{16,18},{18... | collective-permute-start | bytes 1544 | tf_op jit(solution)/shard_map/ppermute | solution.py:13
  2.9 4.1 %collective-permute-start = (s32[4,32]{1,0:T(4,128)}, s32[4,32]{1,0:T(4,128)S(1)}, u32[]{:S(2)}, u32[]{:S(2)}) collective-permute-start(s32[4,32]{1,0:T(4,128)} %param.10), channel_id=1, source_target_pairs={{2,0},{4,2},{6,4},{8,6},{10,8},{12,10},{14,12},{16,14},{18,16},{20... | collective-permute-start | bytes 1544 | tf_op jit(solution)/shard_map/ppermute | solution.py:16
  7.0 0.9 %convert_reduce_fusion.1 = s32[4]{0:T(128)S(1)} fusion(s32[4]{0:T(128)} %bitcast.25), kind=kLoop, calls=%fused_computation.53 | loop fusion | flops 76 | bytes 32 | tf_op jit(solution)/shard_map/reduce_sum | solution.py:63
  7.9 0.7 %multiply_add_fusion = s32[4]{0:T(128)S(1)} fusion(s32[4]{0:T(128)S(1)} %convert_reduce_fusion.1, s32[4,1]{0,1:T(1,128)} %param.15), kind=kLoop, calls=%fused_computation.63 | loop fusion | flops 8 | bytes 48 | tf_op jit(solution)/shard_map/add | solution.py:64
  8.6 0.9 %convolution_convert_fusion.3 = bf16[6,256]{1,0:T(8,128)(2,1)S(1)} fusion(s32[4,256]{1,0:T(4,128)} %param.13, s32[4]{0:T(128)S(1)} %multiply_add_fusion), kind=kOutput, calls=%fused_computation.7 | convolution fusion | flops 76312 | bytes 7184 | tf_op jit(solution)/shard_map/dot_general | solution.py:68
  9.5 0.6 %convert_element_type.41 = bf16[2,3,256]{2,1,0:T(4,128)(2,1)} reshape(bf16[6,256]{1,0:T(8,128)(2,1)S(1)} %convolution_convert_fusion.3) | data formatting | bytes 6144 | tf_op jit(solution)/shard_map/convert_element_type | solution.py:86
  10.1 3.2 %all-to-all-start = ((bf16[2,3,256]{2,1,0:T(4,128)(2,1)}), bf16[2,3,256]{2,1,0:T(4,128)(2,1)S(1)}, u32[]{:S(2)}, u32[]{:S(2)}) async-start(bf16[2,3,256]{2,1,0:T(4,128)(2,1)} %convert_element_type.41), calls=%async_computation | async-start | bytes 8192 | tf_op jit(solution)/shard_map/all_to_all | solution.py:85
  13.3 0.8 %convert_reduce_fusion = f32[4]{0:T(128)S(1)} fusion(s32[4,256]{1,0:T(4,128)} %param.13), kind=kLoop, calls=%fused_computation.27 | loop fusion | flops 2044 | bytes 4112 | tf_op jit(solution)/shard_map/reduce_sum | solution.py:59
  14.1 0.7 %compare_select_fusion.2 = s32[4,32]{1,0:T(4,128)S(1)} fusion(s32[4,32]{1,0:T(4,128)} %param.10), kind=kLoop, calls=%fused_computation.21 | loop fusion | flops 1792 | bytes 1024 | tf_op jit(solution)/shard_map/select_n | solution.py:51
  14.8 0.1 reshape.37
  14.9 0.7 %broadcast_compare_fusion.2 = (pred[4,32]{1,0:T(4,128)(4,1)S(1)}, s32[4,32]{1,0:T(4,128)S(1)}) fusion(s32[]{:T(128)S(6)} %axis_index.15, s32[4,32]{1,0:T(4,128)} %param.10), kind=kLoop, calls=%fused_computation.59 | loop fusion | flops 3712 | bytes 1156 | tf_op jit(solution)/shard_map/eq | solution.py:53
  15.6 0.9 %convolution_convert_fusion.2 = bf16[6,256]{1,0:T(8,128)(2,1)S(1)} fusion(f32[4,256]{1,0:T(4,128)} %param.14, f32[4]{0:T(128)S(1)} %broadcast_add_fusion, s32[4]{0:T(128)S(1)} %multiply_add_fusion), kind=kOutput, calls=%fused_computation.6 | convolution fusion | flops 77336 | bytes 7200 | tf_op jit(solution)/shard_map/dot_general | solution.py:71
  16.6 0.6 %convert_element_type.47 = bf16[2,3,256]{2,1,0:T(4,128)(2,1)} reshape(bf16[6,256]{1,0:T(8,128)(2,1)S(1)} %convolution_convert_fusion.2) | data formatting | bytes 6144 | tf_op jit(solution)/shard_map/convert_element_type | solution.py:90
  17.2 0.7 %convert_element_type.42 = f32[4,4,256]{2,1,0:T(4,128)S(1)} convert(bf16[4,4,256]{2,1,0:T(4,128)(2,1)} %param.12) | non-fusion elementwise | flops 4096 | bytes 24576 | tf_op jit(solution)/shard_map/convert_element_type | solution.py:28
  17.9 0.0 copy-done
  17.9 0.9 %gather_fusion = bf16[128,384]{1,0:T(8,128)(2,1)S(1)} fusion(bf16[4096,384]{1,0:T(8,128)(2,1)S(1)} %copy-done, s32[1024]{0:T(1024)S(1)} %pad_clamp_fusion.2), kind=kCustom, calls=%fused_computation | custom fusion | bytes 197120 | tf_op jit(solution)/shard_map/gather | solution.py:51
  18.8 0.0 all-to-all-done
  18.8 3.2 %all-to-all-start.2 = ((bf16[2,3,256]{2,1,0:T(4,128)(2,1)}), bf16[2,3,256]{2,1,0:T(4,128)(2,1)S(1)}, u32[]{:S(2)}, u32[]{:S(2)}) async-start(bf16[2,3,256]{2,1,0:T(4,128)(2,1)} %convert_element_type.47), calls=%async_computation.2 | async-start | bytes 8192 | tf_op jit(solution)/shard_map/all_to_all | solution.py:89
  22.0 1.3 %all-to-all-done.2 = bf16[2,3,256]{2,1,0:T(4,128)(2,1)S(1)} async-done(((bf16[2,3,256]{2,1,0:T(4,128)(2,1)}), bf16[2,3,256]{2,1,0:T(4,128)(2,1)S(1)}, u32[]{:S(2)}, u32[]{:S(2)}) %all-to-all-start.2) | async-done | bytes 3104 | tf_op jit(solution)/shard_map/all_to_all | solution.py:89
  23.4 0.0 collective-permute-done.2
  23.4 0.1 reshape.53
  23.5 0.0 collective-permute-done
  23.5 0.1 reshape.45
  23.6 0.9 %gather_fusion.1 = bf16[128,384]{1,0:T(8,128)(2,1)S(1)} fusion(bf16[4096,384]{1,0:T(8,128)(2,1)S(1)} %copy-done, s32[1024]{0:T(1024)S(1)} %pad_clamp_fusion.1), kind=kCustom, calls=%fused_computation.1 | custom fusion | bytes 197120 | tf_op jit(solution)/shard_map/gather | solution.py:48
  24.5 0.9 %gather_fusion.2 = bf16[128,384]{1,0:T(8,128)(2,1)S(1)} fusion(bf16[4096,384]{1,0:T(8,128)(2,1)S(1)} %copy-done, s32[1024]{0:T(1024)S(1)} %pad_clamp_fusion), kind=kCustom, calls=%fused_computation.2 | custom fusion | bytes 197120 | tf_op jit(solution)/shard_map/gather | solution.py:47
  25.3 2.0 %collective-permute-start.3 = (bf16[4,32,384]{2,1,0:T(8,128)(2,1)S(1)}, bf16[4,32,384]{2,1,0:T(8,128)(2,1)S(1)}, u32[]{:S(2)}, u32[]{:S(2)}) collective-permute-start(bf16[4,32,384]{2,1,0:T(8,128)(2,1)S(1)} %bitcast.24), channel_id=1, source_target_pairs={{0,30},{2,0},{4,2},{6,4},{8,6},{10,8},{12,10},{14,12},{16,14},{18,... | collective-permute-start | bytes 294920 | tf_op jit(solution)/shard_map/ppermute | solution.py:23
  27.3 0.1 collective-permute-start.1
  27.4 0.8 %select_reduce_fusion = bf16[4,256,32]{1,2,0:T(8,128)(2,1)S(1)} fusion(f32[4,4,256]{2,1,0:T(4,128)S(1)} %convert_element_type.42, s32[4,4,256]{2,1,0:T(4,128)} %param.11), kind=kLoop, calls=%fused_computation.12 | loop fusion | flops 360448 | bytes 98304 | tf_op jit(solution)/shard_map/reduce_sum | solution.py:28
  28.2 2.8 %collective-permute-done.3 = bf16[4,32,384]{2,1,0:T(8,128)(2,1)S(1)} collective-permute-done((bf16[4,32,384]{2,1,0:T(8,128)(2,1)S(1)}, bf16[4,32,384]{2,1,0:T(8,128)(2,1)S(1)}, u32[]{:S(2)}, u32[]{:S(2)}) %collective-permute-start.3) | collective-permute-done | bytes 98336 | tf_op jit(solution)/shard_map/ppermute | solution.py:23
  31.0 4.5 %collective-permute-done.1 = bf16[4,32,384]{2,1,0:T(8,128)(2,1)S(1)} collective-permute-done((bf16[4,32,384]{2,1,0:T(8,128)(2,1)S(1)}, bf16[4,32,384]{2,1,0:T(8,128)(2,1)S(1)}, u32[]{:S(2)}, u32[]{:S(2)}) %collective-permute-start.1) | collective-permute-done | bytes 98336 | tf_op jit(solution)/shard_map/ppermute | solution.py:23
  35.5 0.4 convolution_convert_fusion.1
  36.0 0.9 %convolution_convert_fusion = bf16[6,256,384]{2,0,1:T(8,128)(2,1)S(1)} fusion(bf16[4,256,384]{2,1,0:T(8,128)(2,1)S(1)} %convolution_convert_fusion.1, s32[4]{0:T(128)S(1)} %multiply_add_fusion), kind=kOutput, calls=%fused_computation.4 | convolution fusion | flops 5308440 | bytes 1966096 | tf_op jit(solution)/shard_map/sr,rbx->sbx/dot_general | solution.py:77
  36.9 0.0 copy-start.1
  36.9 0.2 copy.12
  37.0 4.7 %all_to_all.15 = bf16[2,3,256,384]{3,2,1,0:T(8,128)(2,1)S(1)} all-to-all(bf16[2,3,256,384]{3,2,1,0:T(8,128)(2,1)S(1)} %bitcast.21), channel_id=1, replica_groups=mesh['scalp'=16,'screen'=2] {'screen'}, dimensions={0} | all-to-all | bytes 2359296 | tf_op jit(solution)/shard_map/all_to_all | solution.py:81
  41.7 0.0 copy-done.1
  41.7 0.0 copy-start.2
  41.7 1.4 %fusion.2 = f32[1536,768]{1,0:T(8,128)S(1)} fusion(bf16[1536,384]{1,0:T(8,128)(2,1)S(1)} %bitcast.19, bf16[1,384,768]{2,1,0:T(8,128)(2,1)S(1)} %copy-done.1), kind=kOutput, calls=%fused_computation.10 | convolution fusion | flops 905969664 | bytes 6488064 | tf_op jit(solution)/shard_map/dot_general | solution.py:83
  43.1 0.0 copy-done.2
  43.1 2.8 %multiply_convert_fusion = bf16[1536,768]{1,0:T(8,128)(2,1)} fusion(f32[1536,768]{1,0:T(8,128)S(1)} %fusion.2, bf16[1536,384]{1,0:T(8,128)(2,1)S(1)} %bitcast.20, f32[1536]{0:T(1024)S(1)} %reshape.34, f32[1536]{0:T(1024)S(1)} %reshape.33, bf16[1,384,768]{2,1,0:T(8,128)(2,1)S(1)} %copy-done.2), kind=kOutput, calls=%fused_computation.3 | convolution fusion | flops 910688256 | bytes 8859648 | tf_op jit(solution)/shard_map/dot_general | solution.py:84
  (9 shorter events, 0.1 us)
Async XLA Ops:
  0.0 17.9 %copy-start = (bf16[4096,384]{1,0:T(8,128)(2,1)S(1)}, bf16[4096,384]{1,0:T(8,128)(2,1)}, u32[]{:S(2)}) copy-start(bf16[4096,384]{1,0:T(8,128)(2,1)} %param.9) | copy-start | bytes 9437188
  0.0 23.4 %collective-permute-start.2 = (s32[4,32]{1,0:T(4,128)}, s32[4,32]{1,0:T(4,128)S(1)}, u32[]{:S(2)}, u32[]{:S(2)}) collective-permute-start(s32[4,32]{1,0:T(4,128)} %param.10), channel_id=1, source_target_pairs={{0,2},{2,4},{4,6},{6,8},{8,10},{10,12},{12,14},{14,16},{16,18},{18... | collective-permute-start | bytes 1544 | tf_op jit(solution)/shard_map/ppermute | solution.py:13
  2.9 20.5 %collective-permute-start = (s32[4,32]{1,0:T(4,128)}, s32[4,32]{1,0:T(4,128)S(1)}, u32[]{:S(2)}, u32[]{:S(2)}) collective-permute-start(s32[4,32]{1,0:T(4,128)} %param.10), channel_id=1, source_target_pairs={{2,0},{4,2},{6,4},{8,6},{10,8},{12,10},{14,12},{16,14},{18,16},{20... | collective-permute-start | bytes 1544 | tf_op jit(solution)/shard_map/ppermute | solution.py:16
  10.1 8.6 %all-to-all-start = ((bf16[2,3,256]{2,1,0:T(4,128)(2,1)}), bf16[2,3,256]{2,1,0:T(4,128)(2,1)S(1)}, u32[]{:S(2)}, u32[]{:S(2)}) async-start(bf16[2,3,256]{2,1,0:T(4,128)(2,1)} %convert_element_type.41), calls=%async_computation | async-start | bytes 8192 | tf_op jit(solution)/shard_map/all_to_all | solution.py:85
  18.8 4.6 %all-to-all-start.2 = ((bf16[2,3,256]{2,1,0:T(4,128)(2,1)}), bf16[2,3,256]{2,1,0:T(4,128)(2,1)S(1)}, u32[]{:S(2)}, u32[]{:S(2)}) async-start(bf16[2,3,256]{2,1,0:T(4,128)(2,1)} %convert_element_type.47), calls=%async_computation.2 | async-start | bytes 8192 | tf_op jit(solution)/shard_map/all_to_all | solution.py:89
  25.3 5.7 %collective-permute-start.3 = (bf16[4,32,384]{2,1,0:T(8,128)(2,1)S(1)}, bf16[4,32,384]{2,1,0:T(8,128)(2,1)S(1)}, u32[]{:S(2)}, u32[]{:S(2)}) collective-permute-start(bf16[4,32,384]{2,1,0:T(8,128)(2,1)S(1)} %bitcast.24), channel_id=1, source_target_pairs={{0,30},{2,0},{4,2},{6,4},{8,6},{10,8},{12,10},{14,12},{16,14},{18,... | collective-permute-start | bytes 294920 | tf_op jit(solution)/shard_map/ppermute | solution.py:23
  27.3 8.2 %collective-permute-start.1 = (bf16[4,32,384]{2,1,0:T(8,128)(2,1)S(1)}, bf16[4,32,384]{2,1,0:T(8,128)(2,1)S(1)}, u32[]{:S(2)}, u32[]{:S(2)}) collective-permute-start(bf16[4,32,384]{2,1,0:T(8,128)(2,1)S(1)} %bitcast.23), channel_id=1, source_target_pairs={{0,2},{2,4},{4,6},{6,8},{8,10},{10,12},{12,14},{14,16},{16,18},{18... | collective-permute-start | bytes 294920 | tf_op jit(solution)/shard_map/ppermute | solution.py:23
  36.9 4.9 %copy-start.1 = (bf16[1,384,768]{2,1,0:T(8,128)(2,1)S(1)}, bf16[1,384,768]{2,1,0:T(8,128)(2,1)}, u32[]{:S(2)}) copy-start(bf16[1,384,768]{2,1,0:T(8,128)(2,1)} %param.16) | copy-start | bytes 1769476
  41.7 1.4 %copy-start.2 = (bf16[1,384,768]{2,1,0:T(8,128)(2,1)S(1)}, bf16[1,384,768]{2,1,0:T(8,128)(2,1)}, u32[]{:S(2)}) copy-start(bf16[1,384,768]{2,1,0:T(8,128)(2,1)} %param.17) | copy-start | bytes 1769476
where the time goes:
time: 46.5 us; the launch traced here: 45.9 us
  starting transfers between devices  15.5 us (33%)
  waiting for transfers between devices  8.72 us (19%)
  matrix products  7.39 us (16%)
  other arithmetic  5.3 us (11%)
  blocking collectives  4.68 us (10%)
  local copies, waits for them, and re-layouts  4.26 us (9%)
    ppermute x2, waiting for transfers between devices, shifted(): lax.ppermute(x, axis, [(i, (i + by) % devices) for i in range(devices)])  7.38 us
    all_to_all x1, blocking collectives, shards(): lax.all_to_all(panel_packed, 'screen', split_axis=0, concat_axis=0, tiled...  4.68 us
    ppermute x1, starting transfers between devices, extended(): lax.ppermute(lax.slice_in_dim(block, 0, width, axis=dim), axis, backward)  4.05 us
    all_to_all x1, starting transfers between devices, shards(): lax.all_to_all(scaled_packed.astype(jnp.bfloat16), 'screen', split_axis=0...  3.23 us
    all_to_all x1, starting transfers between devices, shards(): lax.all_to_all(kept_packed.astype(jnp.bfloat16), 'screen', split_axis=0,...  3.19 us
    ppermute x1, starting transfers between devices, extended(): lax.ppermute(lax.slice_in_dim(block, block.shape[dim] - width, None, axis...  2.94 us
    dot_general x1, matrix products, shards(): side = jnp.dot(flat, side_map, preferred_element_type=jnp.float32)  2.81 us
    ppermute x2, starting transfers between devices, shifted(): lax.ppermute(x, axis, [(i, (i + by) % devices) for i in range(devices)])  2.07 us
  transfers between devices with their start and end apart: 6, of which 3 were waited for; matrix products, arithmetic and copies ran while one was open for 21% of the time, Pallas kernels for 0%

commit v1 on v0

v1 whole, which is shorter than its diff:
```python
import functools

import jax
import jax.numpy as jnp
from jax import lax
from jax.experimental import pallas as pl
from jax.experimental.pallas import tpu as pltpu
from jax.sharding import PartitionSpec as P

MESH = pl.DeviceIdType.MESH
CHUNK = 512


def columns(lists, lanes):
    parts = []
    for b in range(lists.shape[0]):
        row = jnp.broadcast_to(lists[b : b + 1, :], (lanes, lists.shape[1]))
        parts.append(row.T)
    return jnp.concatenate(parts, axis=0)


def pick_rows(wanted, guides, total):
    rows, lanes = wanted.shape
    tile = guides.shape[0]
    chunk = min(CHUNK, tile)
    lane = lax.broadcasted_iota(jnp.int32, (rows, lanes), 1)
    total[:rows] = jnp.zeros((rows, guides.shape[1]), jnp.float32)

    def body(i, carry):
        base = pl.multiple_of(i * chunk, chunk)
        hit = jnp.concatenate(
            [
                jnp.where(wanted == lane + (base + at), 1.0, 0.0).astype(jnp.bfloat16)
                for at in range(0, chunk, lanes)
            ],
            axis=1,
        )
        total[:rows] += jnp.dot(
            hit, guides[pl.ds(base, chunk), :], preferred_element_type=jnp.float32
        )
        return carry

    lax.fori_loop(0, tile // chunk, body, 0)
    return total[:rows]


def exchange(
    scalps,
    guides_ref,
    near_ref,
    pick_ref,
    weight_ref,
    keep_ref,
    width_ref,
    route_ref,
    rows_ref,
    data_ref,
    tiles_ref,
    guides,
    lists,
    outgoing,
    incoming,
    total,
    local_sem,
    send_sem,
    recv_sem,
):
    here = lax.axis_index("scalp")
    core = lax.axis_index("screen")
    lower = (lax.rem(here + scalps - 1, scalps), core)
    upper = (lax.rem(here + 1, scalps), core)
    pair = (here, 1 - core)
    tile = guides.shape[0]
    blocks, listed = near_ref.shape
    count = blocks * listed
    lanes = 128

    load = pltpu.make_async_copy(guides_ref, guides, local_sem)
    load.start()
    barrier = pltpu.get_barrier_semaphore()
    for other in (lower, upper, pair):
        pl.semaphore_signal(barrier, inc=1, device_id=other, device_id_type=MESH)

    def remote(src, dst, at, to):
        return pltpu.make_async_remote_copy(
            src_ref=src,
            dst_ref=dst,
            send_sem=send_sem.at[at],
            recv_sem=recv_sem.at[at],
            device_id=to,
            device_id_type=MESH,
        )

    kept = keep_ref[...].astype(jnp.float32)
    strands = kept.shape[1]
    scaled = width_ref[...] * strands / (jnp.sum(kept, axis=1, keepdims=True) + 1.0)
    joins = pick_ref.shape[1]
    spare = data_ref.shape[2] - 2 * joins - 2
    for b in range(blocks):
        data_ref[core, b] = jnp.concatenate(
            [
                pick_ref[b].astype(jnp.float32),
                weight_ref[b].astype(jnp.float32),
                kept[b : b + 1],
                (kept * scaled)[b : b + 1],
                jnp.zeros((spare, strands), jnp.float32),
            ],
            axis=0,
        )
    tiles_ref[core] = route_ref[...]
    pl.semaphore_wait(barrier, 3)

    ask_upper = remote(near_ref, lists.at[0], 0, upper)
    ask_lower = remote(near_ref, lists.at[1], 1, lower)
    ask_upper.start()
    ask_lower.start()
    give_data = remote(data_ref.at[core], data_ref.at[core], 2, pair)
    give_data.start()
    give_tiles = remote(tiles_ref.at[core], tiles_ref.at[core], 3, pair)
    give_tiles.start()

    load.wait()
    offset = here * tile
    own = pick_rows(columns(near_ref[...], lanes) - offset, guides, total).astype(jnp.bfloat16)
    rows_ref[core] = own
    ask_upper.wait()
    ask_lower.wait()
    wanted = jnp.concatenate([columns(lists[0], lanes), columns(lists[1], lanes)], axis=0)
    both = pick_rows(wanted - offset, guides, total).astype(jnp.bfloat16)
    outgoing[0] = both[:count]
    outgoing[1] = both[count:]
    to_lower = remote(outgoing.at[0], incoming.at[1], 4, lower)
    to_upper = remote(outgoing.at[1], incoming.at[0], 5, upper)
    to_lower.start()
    to_upper.start()
    to_lower.wait()
    to_upper.wait()
    rows_ref[core] = rows_ref[core] + incoming[0] + incoming[1]
    give_rows = remote(rows_ref.at[core], rows_ref.at[core], 6, pair)
    give_rows.start()
    give_data.wait()
    give_tiles.wait()
    give_rows.wait()


def tessellate(joins, cap, tiles_ref, rows_ref, data_ref, centre_ref, side_ref, out_ref, maps):
    screens, blocks = tiles_ref.shape[:2]
    listed = rows_ref.shape[1] // blocks
    step = pl.program_id(0)

    @pl.when(step == 0)
    def _():
        for c in range(screens):
            for half, table in enumerate((centre_ref, side_ref)):
                made = jnp.dot(
                    rows_ref[c], table[0], preferred_element_type=jnp.float32
                ).astype(jnp.bfloat16)
                for b in range(blocks):
                    maps[c * blocks + b, half * listed : (half + 1) * listed] = made[
                        b * listed : (b + 1) * listed
                    ]

    mine = lax.axis_index("screen")
    source = step // cap
    place = step % cap
    rank = jnp.int32(0)
    block = jnp.int32(0)
    found = jnp.int32(0)
    for b in range(blocks):
        same = (tiles_ref[source, b, 0] == mine).astype(jnp.int32)
        hit = same * (rank == place).astype(jnp.int32)
        block = block + hit * b
        found = found + hit
        rank = rank + same
    data = data_ref[source, block]
    strands = data.shape[1]
    names = lax.broadcasted_iota(jnp.int32, (listed, strands), 0).astype(jnp.float32)
    mix = jnp.zeros((listed, strands), jnp.float32)
    for j in range(joins):
        mix = jnp.where(names == data[j : j + 1], data[joins + j : joins + j + 1], mix)
    mix = mix * found.astype(jnp.float32)
    spread = jnp.concatenate(
        [mix * data[2 * joins : 2 * joins + 1], mix * data[2 * joins + 1 : 2 * joins + 2]], axis=0
    ).astype(jnp.bfloat16)
    out_ref[...] = lax.dot_general(
        spread,
        maps[source * blocks + block],
        (((0,), (0,)), ((), ())),
        preferred_element_type=jnp.float32,
    ).astype(out_ref.dtype)


def shards(guides, neighbours, pick, pick_weight, keep, width, route, tess_centre, tess_side):
    scalps = lax.axis_size("scalp")
    screens = lax.axis_size("screen")
    tile, points = guides.shape
    blocks, listed = neighbours.shape
    strands = keep.shape[1]
    joins = pick.shape[1]
    cap = blocks // screens + blocks // 4
    count = blocks * listed
    fields = -(-(2 * joins + 2) // 8) * 8
    verts = tess_centre.shape[2]
    vmem = pl.BlockSpec(memory_space=pltpu.VMEM)
    rows, data, tiles = pl.pallas_call(
        functools.partial(exchange, scalps),
        out_shape=(
            jax.ShapeDtypeStruct((screens, count, points), jnp.bfloat16),
            jax.ShapeDtypeStruct((screens, blocks, fields, strands), jnp.float32),
            jax.ShapeDtypeStruct((screens, blocks, 1), jnp.int32),
        ),
        in_specs=[pl.BlockSpec(memory_space=pl.ANY)] + [vmem] * 6,
        out_specs=(vmem, vmem, vmem),
        scratch_shapes=[
            pltpu.VMEM((tile, points), jnp.bfloat16),
            pltpu.VMEM((2, blocks, listed), jnp.int32),
            pltpu.VMEM((2, count, points), jnp.bfloat16),
            pltpu.VMEM((2, count, points), jnp.bfloat16),
            pltpu.VMEM((2 * count, points), jnp.float32),
            pltpu.SemaphoreType.DMA,
            pltpu.SemaphoreType.DMA((7,)),
            pltpu.SemaphoreType.DMA((7,)),
        ],
        compiler_params=pltpu.CompilerParams(
            collective_id=0, has_side_effects=True, vmem_limit_bytes=24 * 1024 * 1024
        ),
    )(guides, neighbours, pick, pick_weight, keep, width, route)
    whole = lambda a: pl.BlockSpec(a.shape, lambda i: (0,) * a.ndim)
    return pl.pallas_call(
        functools.partial(tessellate, joins, cap),
        grid=(screens * cap,),
        out_shape=jax.ShapeDtypeStruct((screens * cap * strands, verts), jnp.bfloat16),
        in_specs=[
            pl.BlockSpec(memory_space=pltpu.SMEM),
            whole(rows),
            whole(data),
            whole(tess_centre),
            whole(tess_side),
        ],
        out_specs=pl.BlockSpec((strands, verts), lambda i: (i, 0)),
        scratch_shapes=[pltpu.VMEM((screens * blocks, 2 * listed, verts), jnp.bfloat16)],
        compiler_params=pltpu.CompilerParams(vmem_limit_bytes=24 * 1024 * 1024),
    )(tiles, rows, data, tess_centre, tess_side)


def solution(mesh):
    return jax.shard_map(
        shards,
        mesh=mesh,
        in_specs=(
            P("scalp", None),
            P(("scalp", "screen"), None),
            P(("scalp", "screen"), None, None),
            P(("scalp", "screen"), None, None),
            P(("scalp", "screen"), None),
            P(("scalp", "screen"), None),
            P(("scalp", "screen"), None),
            P("screen", None, None),
            P("screen", None, None),
        ),
        out_specs=P(("scalp", "screen"), None),
        check_vma=False,
    )
```

time: 46.5 us -> 31.9 us (0.69)
  Pallas kernels: 0 us -> 25.4 us
  starting transfers between devices: 15.5 us -> 0 us
  waiting for transfers between devices: 8.72 us -> 0 us
  matrix products: 7.39 us -> 0 us
  other arithmetic: 5.3 us -> 0 us
  blocking collectives: 4.68 us -> 0 us
  local copies, waits for them, and re-layouts: 4.26 us -> 6.1 us
    pallas_call x0 -> x2, Pallas kernels: none -> 25.4 us  [the longest x1 20.6 us: shards(): pl.pallas_call(functools.partial(exchange, scalps), out_shape=(jax.ShapeD...]
    ppermute x4 -> x0, starting transfers between devices: 9.06 us -> none  [the longest x1 4.05 us: extended(): lax.ppermute(lax.slice_in_dim(block, 0, width, axis=dim), axis, backward)]
    dot_general x6 -> x0, matrix products: 7.39 us -> none  [the longest x1 2.81 us: shards(): side = jnp.dot(flat, side_map, preferred_element_type=jnp.float32)]
    ppermute x4 -> x0, waiting for transfers between devices: 7.38 us -> none  [the longest x2 7.38 us: shifted(): lax.ppermute(x, axis, [(i, (i + by) % devices) for i in range(devices)])]
    all_to_all x2 -> x0, starting transfers between devices: 6.43 us -> none  [the longest x1 3.23 us: shards(): lax.all_to_all(scaled_packed.astype(jnp.bfloat16), 'screen', split_axis=0...]
    unnamed x6 -> x17, local copies, waits for them, and re-layouts: 0.01 us -> 6.1 us
    all_to_all x1 -> x0, blocking collectives: 4.68 us -> none  [shards(): lax.all_to_all(panel_packed, 'screen', split_axis=0, concat_axis=0, tiled...]
    gather x3 -> x0, local copies, waits for them, and re-layouts: 2.59 us -> none  [the longest x1 0.86 us: shards(): for_lower = guides[lower_list % tile]]
  transfers between devices with their start and end apart: 6 -> 0, of which waited for: 3 -> 0; matrix products, arithmetic and copies ran while one was open for 21% -> 0% of each run, Pallas kernels for 0% -> 0%
where the time goes in v1:
time: 31.9 us; the launch traced here: 31.6 us
  Pallas kernels  25.4 us (80%)
  local copies, waits for them, and re-layouts  6.1 us (19%)
    pallas_call x1, Pallas kernels, shards(): pl.pallas_call(functools.partial(exchange, scalps), out_shape=(jax.ShapeD...  20.6 us
    unnamed x17, local copies, waits for them, and re-layouts  6.1 us
    pallas_call x1, Pallas kernels, shards(): pl.pallas_call(functools.partial(tessellate, joins, cap), grid=(screens *...  4.81 us

profile of v1, /device:TPU:0, one launch (start us, length us, event | category | flops | bytes accessed | tf_op | source)
XLA Modules:
  0.0 31.6 jit_solution(14123468504010804538)
XLA Ops:
  0.0 0.7 %copy.10.route_ref = s32[4,1]{1,0:T(4,128)S(1)} copy(s32[4,1]{0,1:T(1,128)} %param.15) | data formatting | bytes 32 | tf_op args[6]
  0.7 0.0 copy-start
  0.7 1.9 %copy-done = bf16[4096,384]{1,0:T(8,128)(2,1)S(1)} copy-done((bf16[4096,384]{1,0:T(8,128)(2,1)S(1)}, bf16[4096,384]{1,0:T(8,128)(2,1)}, u32[]{:S(2)}) %copy-start) | copy-done | bytes 3145752
  2.6 0.0 copy-start.3
  2.6 0.7 %copy-done.3 = s32[4,4,256]{2,1,0:T(4,128)S(1)} copy-done((s32[4,4,256]{2,1,0:T(4,128)S(1)}, s32[4,4,256]{2,1,0:T(4,128)}, u32[]{:S(2)}) %copy-start.3) | copy-done | bytes 16408
  3.3 0.0 copy-start.4
  3.4 0.7 %copy-done.4 = bf16[4,4,256]{2,1,0:T(4,128)(2,1)S(1)} copy-done((bf16[4,4,256]{2,1,0:T(4,128)(2,1)S(1)}, bf16[4,4,256]{2,1,0:T(4,128)(2,1)}, u32[]{:S(2)}) %copy-start.4) | copy-done | bytes 8216
  4.0 0.0 copy-start.5
  4.0 0.7 %copy-done.5 = s32[4,256]{1,0:T(4,128)S(1)} copy-done((s32[4,256]{1,0:T(4,128)S(1)}, s32[4,256]{1,0:T(4,128)}, u32[]{:S(2)}) %copy-start.5) | copy-done | bytes 4120
  4.7 0.0 copy-start.6
  4.7 0.7 %copy-done.6 = f32[4,256]{1,0:T(4,128)S(1)} copy-done((f32[4,256]{1,0:T(4,128)S(1)}, f32[4,256]{1,0:T(4,128)}, u32[]{:S(2)}) %copy-start.6) | copy-done | bytes 4120
  5.4 0.0 copy-start.7
  5.4 0.7 %copy-done.7 = s32[4,32]{1,0:T(4,128)S(1)} copy-done((s32[4,32]{1,0:T(4,128)S(1)}, s32[4,32]{1,0:T(4,128)}, u32[]{:S(2)}) %copy-start.7) | copy-done | bytes 536
  6.1 0.0 copy-start.1
  6.1 0.0 copy-start.2
  6.1 20.6 %shard_map.91 = (bf16[2,128,384]{2,1,0:T(8,128)(2,1)S(1)}, f32[2,4,16,256]{3,2,1,0:T(8,128)S(1)}, s32[2,4,1]{2,1,0:T(4,128)S(1)}) custom-call(bf16[4096,384]{1,0:T(8,128)(2,1)S(1)} %copy-done, s32[4,32]{1,0:T(4,128)S(1)} %copy-done.7, s32[4,4,256]{2,1,0:T(4,128)S(1)} %copy-done.3, bf16[4,4,256]{2,1,0:T(4,128)(2,1)S(1)} %copy-done.4, s32[4,256]{1,0:T(4,128)S(1)} %copy-done.5, ...), custom_call_target="tpu_custom_call" | custom-call | tf_op jit(solution)/shard_map/pallas_call | solution.py:205
  26.7 0.0 copy-done.1
  26.8 0.0 copy-done.2
  26.8 4.8 %shard_map.92 = bf16[1536,768]{1,0:T(8,128)(2,1)} custom-call(s32[2,4,1]{2,1,0:T(4,128)S(1)} %get-tuple-element.8.tiles_ref, bf16[2,128,384]{2,1,0:T(8,128)(2,1)S(1)} %get-tuple-element.9.rows_ref, f32[2,4,16,256]{3,2,1,0:T(8,128)S(1)} %get-tuple-element.10.data_ref, bf16[1,384,768]{2,1,0:T(8,128)(2,1)S(1)} %copy-done.1, bf16[1,384,768]{2,1,0:T(8,128)(2,1)S(1)} %copy-done.2), custom_call_target="tpu_custom_call" | custom-call | tf_op jit(solution)/shard_map/pallas_call | solution.py:229
Async XLA Ops:
  0.7 1.9 %copy-start = (bf16[4096,384]{1,0:T(8,128)(2,1)S(1)}, bf16[4096,384]{1,0:T(8,128)(2,1)}, u32[]{:S(2)}) copy-start(bf16[4096,384]{1,0:T(8,128)(2,1)} %guides_ref.1) | copy-start | bytes 9437188
  2.6 0.7 %copy-start.3 = (s32[4,4,256]{2,1,0:T(4,128)S(1)}, s32[4,4,256]{2,1,0:T(4,128)}, u32[]{:S(2)}) copy-start(s32[4,4,256]{2,1,0:T(4,128)} %pick_ref.1) | copy-start | bytes 49156
  3.3 0.7 %copy-start.4 = (bf16[4,4,256]{2,1,0:T(4,128)(2,1)S(1)}, bf16[4,4,256]{2,1,0:T(4,128)(2,1)}, u32[]{:S(2)}) copy-start(bf16[4,4,256]{2,1,0:T(4,128)(2,1)} %weight_ref.1) | copy-start | bytes 24580
  4.0 0.7 %copy-start.5 = (s32[4,256]{1,0:T(4,128)S(1)}, s32[4,256]{1,0:T(4,128)}, u32[]{:S(2)}) copy-start(s32[4,256]{1,0:T(4,128)} %keep_ref.1) | copy-start | bytes 12292
  4.7 0.7 %copy-start.6 = (f32[4,256]{1,0:T(4,128)S(1)}, f32[4,256]{1,0:T(4,128)}, u32[]{:S(2)}) copy-start(f32[4,256]{1,0:T(4,128)} %width_ref.1) | copy-start | bytes 12292
  5.4 0.7 %copy-start.7 = (s32[4,32]{1,0:T(4,128)S(1)}, s32[4,32]{1,0:T(4,128)}, u32[]{:S(2)}) copy-start(s32[4,32]{1,0:T(4,128)} %near_ref.1) | copy-start | bytes 1540
  6.1 20.6 %copy-start.1 = (bf16[1,384,768]{2,1,0:T(8,128)(2,1)S(1)}, bf16[1,384,768]{2,1,0:T(8,128)(2,1)}, u32[]{:S(2)}) copy-start(bf16[1,384,768]{2,1,0:T(8,128)(2,1)} %centre_ref.1) | copy-start | bytes 1769476
  6.1 20.6 %copy-start.2 = (bf16[1,384,768]{2,1,0:T(8,128)(2,1)S(1)}, bf16[1,384,768]{2,1,0:T(8,128)(2,1)}, u32[]{:S(2)}) copy-start(bf16[1,384,768]{2,1,0:T(8,128)(2,1)} %side_ref.1) | copy-start | bytes 1769476

commit v2 on v1

v2 whole, which is shorter than its diff:
```python
import functools

import jax
import jax.numpy as jnp
from jax import lax
from jax.experimental import pallas as pl
from jax.experimental.pallas import tpu as pltpu
from jax.sharding import PartitionSpec as P

MESH = pl.DeviceIdType.MESH
CHUNK = 1024


def columns(lists, lanes):
    parts = []
    for b in range(lists.shape[0]):
        row = jnp.broadcast_to(lists[b : b + 1, :], (lanes, lists.shape[1]))
        parts.append(row.T)
    return jnp.concatenate(parts, axis=0)


def pick_rows(wanted, guides, total):
    rows, lanes = wanted.shape
    tile = guides.shape[0]
    chunk = min(CHUNK, tile)
    lane = lax.broadcasted_iota(jnp.int32, (rows, lanes), 1)
    total[:rows] = jnp.zeros((rows, guides.shape[1]), jnp.float32)

    def body(i, carry):
        base = pl.multiple_of(i * chunk, chunk)
        hit = jnp.concatenate(
            [
                jnp.where(wanted == lane + (base + at), 1.0, 0.0).astype(jnp.bfloat16)
                for at in range(0, chunk, lanes)
            ],
            axis=1,
        )
        total[:rows] += jnp.dot(
            hit, guides[pl.ds(base, chunk), :], preferred_element_type=jnp.float32
        )
        return carry

    lax.fori_loop(0, tile // chunk, body, 0)
    return total[:rows].astype(jnp.bfloat16)


def exchange(
    scalps,
    guides_hbm,
    near_hbm,
    pick_hbm,
    weight,
    keep_hbm,
    width_hbm,
    route_hbm,
    centre_hbm,
    side_hbm,
    maps,
    spreads,
    tiles,
    guides,
    near,
    pick,
    keep,
    width,
    route,
    centre,
    side,
    rows,
    data,
    lists,
    outgoing,
    incoming,
    total,
    local_sem,
    send_sem,
    recv_sem,
):
    here = lax.axis_index("scalp")
    core = lax.axis_index("screen")
    lower = (lax.rem(here + scalps - 1, scalps), core)
    upper = (lax.rem(here + 1, scalps), core)
    pair = (here, 1 - core)
    tile = guides.shape[0]
    blocks, listed = near.shape
    joins, strands = pick.shape[1:]
    screens = data.shape[0]
    lanes = 128

    barrier = pltpu.get_barrier_semaphore()
    for other in (lower, upper, pair):
        pl.semaphore_signal(barrier, inc=1, device_id=other, device_id_type=MESH)
    loads = [
        pltpu.make_async_copy(src, dst, local_sem.at[at])
        for at, (src, dst) in enumerate(
            (
                (near_hbm, near),
                (pick_hbm, pick),
                (keep_hbm, keep),
                (width_hbm, width),
                (route_hbm, route),
                (guides_hbm, guides),
                (centre_hbm, centre),
                (side_hbm, side),
            )
        )
    ]
    for load in loads:
        load.start()

    def remote(src, dst, at, to):
        return pltpu.make_async_remote_copy(
            src_ref=src,
            dst_ref=dst,
            send_sem=send_sem.at[at],
            recv_sem=recv_sem.at[at],
            device_id=to,
            device_id_type=MESH,
        )

    loads[0].wait()
    pl.semaphore_wait(barrier, 3)
    ask_upper = remote(near, lists.at[0], 0, upper)
    ask_lower = remote(near, lists.at[1], 1, lower)
    ask_upper.start()
    ask_lower.start()

    for load in loads[1:5]:
        load.wait()
    kept = keep[...].astype(jnp.float32)
    scaled = width[...] * strands / (jnp.sum(kept, axis=1, keepdims=True) + 1.0)
    spare = data.shape[2] - 2 * joins - 2
    for b in range(blocks):
        data[core, b] = jnp.concatenate(
            [
                pick[b].astype(jnp.float32),
                weight[b].astype(jnp.float32),
                kept[b : b + 1],
                (kept * scaled)[b : b + 1],
                jnp.zeros((spare, strands), jnp.float32),
            ],
            axis=0,
        )
    tiles[core] = route[...]
    give_data = remote(data.at[core], data.at[core], 2, pair)
    give_data.start()
    give_tiles = remote(tiles.at[core], tiles.at[core], 3, pair)
    give_tiles.start()

    loads[5].wait()
    offset = here * tile
    ask_upper.wait()
    outgoing[0] = pick_rows(columns(lists[0], lanes) - offset, guides, total)
    to_lower = remote(outgoing.at[0], incoming.at[1], 4, lower)
    to_lower.start()
    ask_lower.wait()
    outgoing[1] = pick_rows(columns(lists[1], lanes) - offset, guides, total)
    to_upper = remote(outgoing.at[1], incoming.at[0], 5, upper)
    to_upper.start()

    rows[core] = pick_rows(columns(near[...], lanes) - offset, guides, total)
    give_data.wait()
    give_tiles.wait()
    names = lax.broadcasted_iota(jnp.int32, (listed, strands), 0).astype(jnp.float32)

    def mixing(at, carry):
        fields = data[at // blocks, at % blocks]
        mix = jnp.zeros((listed, strands), jnp.float32)
        for j in range(joins):
            mix = jnp.where(names == fields[j : j + 1], fields[joins + j : joins + j + 1], mix)
        spread = jnp.concatenate(
            [
                mix * fields[2 * joins : 2 * joins + 1],
                mix * fields[2 * joins + 1 : 2 * joins + 2],
            ],
            axis=0,
        )
        spreads[at] = spread.T.astype(jnp.bfloat16)
        return carry

    lax.fori_loop(0, screens * blocks, mixing, 0)
    loads[6].wait()
    loads[7].wait()
    to_lower.wait()
    to_upper.wait()
    rows[core] = rows[core] + incoming[0] + incoming[1]
    give_rows = remote(rows.at[core], rows.at[core], 6, pair)
    give_rows.start()

    def mapped(c):
        for half, table in enumerate((centre, side)):
            made = jnp.dot(rows[c], table[0], preferred_element_type=jnp.float32)
            made = made.astype(jnp.bfloat16)
            for b in range(blocks):
                maps[c, b, half * listed : (half + 1) * listed] = made[
                    b * listed : (b + 1) * listed
                ]

    mapped(core)
    give_rows.wait()
    mapped(1 - core)


def tessellate(cap, tiles, maps, spreads, out, held, sems):
    screens, blocks = maps.shape[:2]
    strands = spreads.shape[1]
    mine = lax.axis_index("screen")
    copies = []
    for source in range(screens):
        for place in range(cap):
            rank = jnp.int32(0)
            block = jnp.int32(0)
            found = jnp.int32(0)
            for b in range(blocks):
                same = (tiles[source, 0, b] == mine).astype(jnp.int32)
                hit = same * (rank == place).astype(jnp.int32)
                block = block + hit * b
                found = found + hit
                rank = rank + same
            slot = source * cap + place
            spread = spreads[source * blocks + block] * found.astype(jnp.float32).astype(
                jnp.bfloat16
            )
            held[slot] = jnp.dot(
                spread, maps[source, block], preferred_element_type=jnp.float32
            ).astype(out.dtype)
            copy = pltpu.make_async_copy(
                held.at[slot], out.at[pl.ds(slot * strands, strands)], sems.at[slot]
            )
            copy.start()
            copies.append(copy)
    for copy in copies:
        copy.wait()


def shards(guides, neighbours, pick, pick_weight, keep, width, route, tess_centre, tess_side):
    scalps = lax.axis_size("scalp")
    screens = lax.axis_size("screen")
    tile, points = guides.shape
    blocks, listed = neighbours.shape
    strands = keep.shape[1]
    joins = pick.shape[1]
    cap = blocks // screens + blocks // 4
    count = blocks * listed
    fields = -(-(2 * joins + 2) // 8) * 8
    verts = tess_centre.shape[2]
    vmem = pl.BlockSpec(memory_space=pltpu.VMEM)
    hbm = pl.BlockSpec(memory_space=pltpu.HBM)
    route = route.reshape(1, blocks)
    maps, spreads, tiles = pl.pallas_call(
        functools.partial(exchange, scalps),
        out_shape=(
            jax.ShapeDtypeStruct((screens, blocks, 2 * listed, verts), jnp.bfloat16),
            jax.ShapeDtypeStruct((screens * blocks, strands, 2 * listed), jnp.bfloat16),
            jax.ShapeDtypeStruct((screens, 1, blocks), jnp.int32),
        ),
        in_specs=[hbm, hbm, hbm, vmem, hbm, hbm, hbm, hbm, hbm],
        out_specs=(vmem, vmem, vmem),
        scratch_shapes=[
            pltpu.VMEM(guides.shape, guides.dtype),
            pltpu.VMEM(neighbours.shape, jnp.int32),
            pltpu.VMEM(pick.shape, jnp.int32),
            pltpu.VMEM(keep.shape, jnp.int32),
            pltpu.VMEM(width.shape, jnp.float32),
            pltpu.VMEM(route.shape, jnp.int32),
            pltpu.VMEM(tess_centre.shape, jnp.bfloat16),
            pltpu.VMEM(tess_side.shape, jnp.bfloat16),
            pltpu.VMEM((screens, count, points), jnp.bfloat16),
            pltpu.VMEM((screens, blocks, fields, strands), jnp.float32),
            pltpu.VMEM((2, blocks, listed), jnp.int32),
            pltpu.VMEM((2, count, points), jnp.bfloat16),
            pltpu.VMEM((2, count, points), jnp.bfloat16),
            pltpu.VMEM((count, points), jnp.float32),
            pltpu.SemaphoreType.DMA((8,)),
            pltpu.SemaphoreType.DMA((7,)),
            pltpu.SemaphoreType.DMA((7,)),
        ],
        compiler_params=pltpu.CompilerParams(
            collective_id=0, has_side_effects=True, vmem_limit_bytes=24 * 1024 * 1024
        ),
    )(guides, neighbours, pick, pick_weight, keep, width, route, tess_centre, tess_side)
    return pl.pallas_call(
        functools.partial(tessellate, cap),
        out_shape=jax.ShapeDtypeStruct((screens * cap * strands, verts), jnp.bfloat16),
        in_specs=[pl.BlockSpec(memory_space=pltpu.SMEM), vmem, vmem],
        out_specs=hbm,
        scratch_shapes=[
            pltpu.VMEM((screens * cap, strands, verts), jnp.bfloat16),
            pltpu.SemaphoreType.DMA((screens * cap,)),
        ],
        compiler_params=pltpu.CompilerParams(vmem_limit_bytes=24 * 1024 * 1024),
    )(tiles, maps, spreads)


def solution(mesh):
    return jax.shard_map(
        shards,
        mesh=mesh,
        in_specs=(
            P("scalp", None),
            P(("scalp", "screen"), None),
            P(("scalp", "screen"), None, None),
            P(("scalp", "screen"), None, None),
            P(("scalp", "screen"), None),
            P(("scalp", "screen"), None),
            P(("scalp", "screen"), None),
            P("screen", None, None),
            P("screen", None, None),
        ),
        out_specs=P(("scalp", "screen"), None),
        check_vma=False,
    )
```

time: 31.9 us -> 30.4 us (0.953)
  Pallas kernels: 25.4 us -> 21.9 us
  local copies, waits for them, and re-layouts: 6.1 us -> 8.14 us
    pallas_call x1, Pallas kernels: 4.81 us -> 2.28 us  [shards(): pl.pallas_call(functools.partial(tessellate, cap), out_shape=jax.ShapeDty...]
    unnamed x17 -> x18, local copies, waits for them, and re-layouts: 6.1 us -> 8.14 us
    pallas_call x1, Pallas kernels: 20.6 us -> 19.6 us  [shards(): pl.pallas_call(functools.partial(exchange, scalps), out_shape=(jax.ShapeD...]
where the time goes in v2:
time: 30.4 us; the launch traced here: 30 us
  Pallas kernels  21.9 us (72%)
  local copies, waits for them, and re-layouts  8.14 us (27%)
    pallas_call x1, Pallas kernels, shards(): pl.pallas_call(functools.partial(exchange, scalps), out_shape=(jax.ShapeD...  19.6 us
    unnamed x18, local copies, waits for them, and re-layouts  8.14 us
    pallas_call x1, Pallas kernels, shards(): pl.pallas_call(functools.partial(tessellate, cap), out_shape=jax.ShapeDty...  2.28 us

profile of v2, /device:TPU:0, one launch (start us, length us, event | category | flops | bytes accessed | tf_op | source)
XLA Modules:
  0.0 30.0 jit_solution(7283258310907199030)
XLA Ops:
  0.0 0.0 copy-start
  0.0 1.9 %copy-done = bf16[4096,384]{1,0:T(8,128)(2,1)S(1)} copy-done((bf16[4096,384]{1,0:T(8,128)(2,1)S(1)}, bf16[4096,384]{1,0:T(8,128)(2,1)}, u32[]{:S(2)}) %copy-start) | copy-done | bytes 3145752
  1.9 0.0 copy-start.1
  1.9 1.1 %copy-done.1 = bf16[1,384,768]{2,1,0:T(8,128)(2,1)S(1)} copy-done((bf16[1,384,768]{2,1,0:T(8,128)(2,1)S(1)}, bf16[1,384,768]{2,1,0:T(8,128)(2,1)}, u32[]{:S(2)}) %copy-start.1) | copy-done | bytes 589848
  3.0 0.0 copy-start.2
  3.0 1.1 %copy-done.2 = bf16[1,384,768]{2,1,0:T(8,128)(2,1)S(1)} copy-done((bf16[1,384,768]{2,1,0:T(8,128)(2,1)S(1)}, bf16[1,384,768]{2,1,0:T(8,128)(2,1)}, u32[]{:S(2)}) %copy-start.2) | copy-done | bytes 589848
  4.0 0.0 copy-start.3
  4.0 0.7 %copy-done.3 = s32[4,4,256]{2,1,0:T(4,128)S(1)} copy-done((s32[4,4,256]{2,1,0:T(4,128)S(1)}, s32[4,4,256]{2,1,0:T(4,128)}, u32[]{:S(2)}) %copy-start.3) | copy-done | bytes 16408
  4.7 0.0 copy-start.4
  4.7 0.7 %copy-done.4 = bf16[4,4,256]{2,1,0:T(4,128)(2,1)S(1)} copy-done((bf16[4,4,256]{2,1,0:T(4,128)(2,1)S(1)}, bf16[4,4,256]{2,1,0:T(4,128)(2,1)}, u32[]{:S(2)}) %copy-start.4) | copy-done | bytes 8216
  5.4 0.0 copy-start.5
  5.4 0.7 %copy-done.5 = s32[4,256]{1,0:T(4,128)S(1)} copy-done((s32[4,256]{1,0:T(4,128)S(1)}, s32[4,256]{1,0:T(4,128)}, u32[]{:S(2)}) %copy-start.5) | copy-done | bytes 4120
  6.1 0.0 copy-start.6
  6.1 0.7 %copy-done.6 = f32[4,256]{1,0:T(4,128)S(1)} copy-done((f32[4,256]{1,0:T(4,128)S(1)}, f32[4,256]{1,0:T(4,128)}, u32[]{:S(2)}) %copy-start.6) | copy-done | bytes 4120
  6.8 0.0 copy-start.7
  6.8 0.7 %copy-done.7 = s32[4,32]{1,0:T(4,128)S(1)} copy-done((s32[4,32]{1,0:T(4,128)S(1)}, s32[4,32]{1,0:T(4,128)}, u32[]{:S(2)}) %copy-start.7) | copy-done | bytes 536
  7.5 0.0 copy-start.8
  7.5 0.7 %copy-done.8 = s32[4,1]{0,1:T(1,128)S(1)} copy-done((s32[4,1]{0,1:T(1,128)S(1)}, s32[4,1]{0,1:T(1,128)}, u32[]{:S(2)}) %copy-start.8) | copy-done | bytes 40
  8.1 19.6 %shard_map.91 = (bf16[2,4,64,768]{3,2,1,0:T(8,128)(2,1)S(1)}, bf16[8,256,64]{2,1,0:T(8,128)(2,1)S(1)}, s32[2,1,4]{2,1,0:T(1,128)S(1)}) custom-call(bf16[4096,384]{1,0:T(8,128)(2,1)S(1)} %copy-done, s32[4,32]{1,0:T(4,128)S(1)} %copy-done.7, s32[4,4,256]{2,1,0:T(4,128)S(1)} %copy-done.3, bf16[4,4,256]{2,1,0:T(4,128)(2,1)S(1)} %copy-done.4, ...), custom_call_target="tpu_custom_call" | custom-call | tf_op jit(solution)/shard_map/pallas_call | solution.py:250
  27.7 2.3 %shard_map.92 = bf16[1536,768]{1,0:T(8,128)(2,1)} custom-call(s32[2,1,4]{2,1,0:T(1,128)S(1)} %get-tuple-element.8.tiles, bf16[2,4,64,768]{3,2,1,0:T(8,128)(2,1)S(1)} %get-tuple-element.9.maps, bf16[8,256,64]{2,1,0:T(8,128)(2,1)S(1)} %get-tuple-element.10.spreads), custom_call_target="tpu_custom_call" | custom-call | tf_op jit(solution)/shard_map/pallas_call | solution.py:282
Async XLA Ops:
  0.0 1.9 %copy-start = (bf16[4096,384]{1,0:T(8,128)(2,1)S(1)}, bf16[4096,384]{1,0:T(8,128)(2,1)}, u32[]{:S(2)}) copy-start(bf16[4096,384]{1,0:T(8,128)(2,1)} %guides_hbm.1) | copy-start | bytes 9437188
  1.9 1.1 %copy-start.1 = (bf16[1,384,768]{2,1,0:T(8,128)(2,1)S(1)}, bf16[1,384,768]{2,1,0:T(8,128)(2,1)}, u32[]{:S(2)}) copy-start(bf16[1,384,768]{2,1,0:T(8,128)(2,1)} %centre_hbm.1) | copy-start | bytes 1769476
  3.0 1.1 %copy-start.2 = (bf16[1,384,768]{2,1,0:T(8,128)(2,1)S(1)}, bf16[1,384,768]{2,1,0:T(8,128)(2,1)}, u32[]{:S(2)}) copy-start(bf16[1,384,768]{2,1,0:T(8,128)(2,1)} %side_hbm.1) | copy-start | bytes 1769476
  4.0 0.7 %copy-start.3 = (s32[4,4,256]{2,1,0:T(4,128)S(1)}, s32[4,4,256]{2,1,0:T(4,128)}, u32[]{:S(2)}) copy-start(s32[4,4,256]{2,1,0:T(4,128)} %pick_hbm.1) | copy-start | bytes 49156
  4.7 0.7 %copy-start.4 = (bf16[4,4,256]{2,1,0:T(4,128)(2,1)S(1)}, bf16[4,4,256]{2,1,0:T(4,128)(2,1)}, u32[]{:S(2)}) copy-start(bf16[4,4,256]{2,1,0:T(4,128)(2,1)} %weight.1) | copy-start | bytes 24580
  5.4 0.7 %copy-start.5 = (s32[4,256]{1,0:T(4,128)S(1)}, s32[4,256]{1,0:T(4,128)}, u32[]{:S(2)}) copy-start(s32[4,256]{1,0:T(4,128)} %keep_hbm.1) | copy-start | bytes 12292
  6.1 0.7 %copy-start.6 = (f32[4,256]{1,0:T(4,128)S(1)}, f32[4,256]{1,0:T(4,128)}, u32[]{:S(2)}) copy-start(f32[4,256]{1,0:T(4,128)} %width_hbm.1) | copy-start | bytes 12292
  6.8 0.7 %copy-start.7 = (s32[4,32]{1,0:T(4,128)S(1)}, s32[4,32]{1,0:T(4,128)}, u32[]{:S(2)}) copy-start(s32[4,32]{1,0:T(4,128)} %near_hbm.1) | copy-start | bytes 1540
  7.5 0.7 %copy-start.8 = (s32[4,1]{0,1:T(1,128)S(1)}, s32[4,1]{0,1:T(1,128)}, u32[]{:S(2)}) copy-start(s32[4,1]{0,1:T(1,128)} %param.15) | copy-start | bytes 52

commit v3 on v2

--- a/solution.py
+++ b/solution.py
@@ -55,6 +55,9 @@
     route_hbm,
     centre_hbm,
     side_hbm,
+    maps_hbm,
+    spreads_hbm,
+    tiles_hbm,
     maps,
     spreads,
     tiles,
@@ -179,6 +182,10 @@
         return carry
 
     lax.fori_loop(0, screens * blocks, mixing, 0)
+    keep_tiles = pltpu.make_async_copy(tiles, tiles_hbm, local_sem.at[8])
+    keep_tiles.start()
+    keep_spreads = pltpu.make_async_copy(spreads, spreads_hbm, local_sem.at[9])
+    keep_spreads.start()
     loads[6].wait()
     loads[7].wait()
     to_lower.wait()
@@ -197,16 +204,39 @@
                 ]
 
     mapped(core)
+    keep_own = pltpu.make_async_copy(maps.at[core], maps_hbm.at[core], local_sem.at[10])
+    keep_own.start()
     give_rows.wait()
     mapped(1 - core)
-
-
-def tessellate(cap, tiles, maps, spreads, out, held, sems):
+    keep_other = pltpu.make_async_copy(
+        maps.at[1 - core], maps_hbm.at[1 - core], local_sem.at[11]
+    )
+    keep_other.start()
+    keep_tiles.wait()
+    keep_spreads.wait()
+    keep_own.wait()
+    keep_other.wait()
+
+
+def tessellate(
+    cap, tiles_hbm, maps_hbm, spreads_hbm, out, tiles, maps, spreads, held, load_sems, sems
+):
     screens, blocks = maps.shape[:2]
     strands = spreads.shape[1]
     mine = lax.axis_index("screen")
+    load_tiles = pltpu.make_async_copy(tiles_hbm, tiles, load_sems.at[0])
+    load_spreads = pltpu.make_async_copy(spreads_hbm, spreads, load_sems.at[1])
+    load_maps = [
+        pltpu.make_async_copy(maps_hbm.at[c], maps.at[c], load_sems.at[2 + c])
+        for c in range(screens)
+    ]
+    for load in [load_tiles, load_spreads] + load_maps:
+        load.start()
+    load_tiles.wait()
+    load_spreads.wait()
     copies = []
     for source in range(screens):
+        load_maps[source].wait()
         for place in range(cap):
             rank = jnp.int32(0)
             block = jnp.int32(0)
@@ -255,8 +285,11 @@
             jax.ShapeDtypeStruct((screens, 1, blocks), jnp.int32),
         ),
         in_specs=[hbm, hbm, hbm, vmem, hbm, hbm, hbm, hbm, hbm],
-        out_specs=(vmem, vmem, vmem),
+        out_specs=(hbm, hbm, hbm),
         scratch_shapes=[
+            pltpu.VMEM((screens, blocks, 2 * listed, verts), jnp.bfloat16),
+            pltpu.VMEM((screens * blocks, strands, 2 * listed), jnp.bfloat16),
+            pltpu.VMEM((screens, 1, blocks), jnp.int32),
             pltpu.VMEM(guides.shape, guides.dtype),
             pltpu.VMEM(neighbours.shape, jnp.int32),
             pltpu.VMEM(pick.shape, jnp.int32),
@@ -271,24 +304,28 @@
             pltpu.VMEM((2, count, points), jnp.bfloat16),
             pltpu.VMEM((2, count, points), jnp.bfloat16),
             pltpu.VMEM((count, points), jnp.float32),
-            pltpu.SemaphoreType.DMA((8,)),
+            pltpu.SemaphoreType.DMA((12,)),
             pltpu.SemaphoreType.DMA((7,)),
             pltpu.SemaphoreType.DMA((7,)),
         ],
         compiler_params=pltpu.CompilerParams(
-            collective_id=0, has_side_effects=True, vmem_limit_bytes=24 * 1024 * 1024
+            collective_id=0, has_side_effects=True, vmem_limit_bytes=56 * 1024 * 1024
         ),
     )(guides, neighbours, pick, pick_weight, keep, width, route, tess_centre, tess_side)
     return pl.pallas_call(
         functools.partial(tessellate, cap),
         out_shape=jax.ShapeDtypeStruct((screens * cap * strands, verts), jnp.bfloat16),
-        in_specs=[pl.BlockSpec(memory_space=pltpu.SMEM), vmem, vmem],
+        in_specs=[hbm, hbm, hbm],
         out_specs=hbm,
         scratch_shapes=[
+            pltpu.SMEM((screens, 1, blocks), jnp.int32),
+            pltpu.VMEM(maps.shape, jnp.bfloat16),
+            pltpu.VMEM(spreads.shape, jnp.bfloat16),
             pltpu.VMEM((screens * cap, strands, verts), jnp.bfloat16),
+            pltpu.SemaphoreType.DMA((2 + screens,)),
             pltpu.SemaphoreType.DMA((screens * cap,)),
         ],
-        compiler_params=pltpu.CompilerParams(vmem_limit_bytes=24 * 1024 * 1024),
+        compiler_params=pltpu.CompilerParams(vmem_limit_bytes=56 * 1024 * 1024),
     )(tiles, maps, spreads)
 
 

time: 30.4 us -> 24.3 us (0.80)
  local copies, waits for them, and re-layouts: 8.14 us -> 0 us
  Pallas kernels: 21.9 us -> 24.1 us
    unnamed x18 -> x0, local copies, waits for them, and re-layouts: 8.14 us -> none
    pallas_call x1, Pallas kernels: 19.6 us -> 21.1 us  [shards(): pl.pallas_call(functools.partial(exchange, scalps), out_shape=(jax.ShapeD...]
    pallas_call x1, Pallas kernels: 2.28 us -> 3.01 us  [shards(): pl.pallas_call(functools.partial(tessellate, cap), out_shape=jax.ShapeDty...]
where the time goes in v3:
time: 24.3 us; the launch traced here: 24.1 us
  Pallas kernels  24.1 us (99%)
    pallas_call x1, Pallas kernels, shards(): pl.pallas_call(functools.partial(exchange, scalps), out_shape=(jax.ShapeD...  21.1 us
    pallas_call x1, Pallas kernels, shards(): pl.pallas_call(functools.partial(tessellate, cap), out_shape=jax.ShapeDty...  3.01 us

profile of v3, /device:TPU:0, one launch (start us, length us, event | category | flops | bytes accessed | tf_op | source)
XLA Modules:
  0.0 24.1 jit_solution(18348872181621837848)
XLA Ops:
  0.0 21.1 %shard_map.91 = (bf16[2,4,64,768]{3,2,1,0:T(8,128)(2,1)}, bf16[8,256,64]{2,1,0:T(8,128)(2,1)}, s32[2,1,4]{2,1,0:T(1,128)}) custom-call(bf16[4096,384]{1,0:T(8,128)(2,1)} %guides_hbm.1, s32[4,32]{1,0:T(4,128)} %near_hbm.1, s32[4,4,256]{2,1,0:T(4,128)} %pick_hbm.1, bf16[4,4,256]{2,1,0:T(4,128)(2,1)} %weight.1, s32[4,256]{1,0:T(4,128)} %keep_hbm.1, ...), custom_call_target="tpu_custom_call" | custom-call | tf_op jit(solution)/shard_map/pallas_call | solution.py:280
  21.1 3.0 %shard_map.92 = bf16[1536,768]{1,0:T(8,128)(2,1)} custom-call(s32[2,1,4]{2,1,0:T(1,128)} %get-tuple-element.8.tiles_hbm, bf16[2,4,64,768]{3,2,1,0:T(8,128)(2,1)} %get-tuple-element.9.maps_hbm, bf16[8,256,64]{2,1,0:T(8,128)(2,1)} %get-tuple-element.10.spreads_hbm), custom_call_target="tpu_custom_call" | custom-call | tf_op jit(solution)/shard_map/pallas_call | solution.py:315

commit v4 on v3

--- a/solution.py
+++ b/solution.py
@@ -24,14 +24,17 @@
     tile = guides.shape[0]
     chunk = min(CHUNK, tile)
     lane = lax.broadcasted_iota(jnp.int32, (rows, lanes), 1)
+    high = wanted >> (lanes.bit_length() - 1)
+    low = jnp.where((wanted & (lanes - 1)) == lane, 1.0, 0.0).astype(jnp.bfloat16)
     total[:rows] = jnp.zeros((rows, guides.shape[1]), jnp.float32)
 
     def body(i, carry):
         base = pl.multiple_of(i * chunk, chunk)
+        group = (high - i * (chunk // lanes)).astype(jnp.float32).astype(jnp.bfloat16)
         hit = jnp.concatenate(
             [
-                jnp.where(wanted == lane + (base + at), 1.0, 0.0).astype(jnp.bfloat16)
-                for at in range(0, chunk, lanes)
+                jnp.where(group == jnp.bfloat16(at), low, jnp.bfloat16(0))
+                for at in range(chunk // lanes)
             ],
             axis=1,
         )
@@ -49,7 +52,7 @@
     guides_hbm,
     near_hbm,
     pick_hbm,
-    weight,
+    weight_hbm,
     keep_hbm,
     width_hbm,
     route_hbm,
@@ -64,6 +67,7 @@
     guides,
     near,
     pick,
+    weight,
     keep,
     width,
     route,
@@ -105,6 +109,7 @@
                 (guides_hbm, guides),
                 (centre_hbm, centre),
                 (side_hbm, side),
+                (weight_hbm, weight),
             )
         )
     ]
@@ -128,7 +133,7 @@
     ask_upper.start()
     ask_lower.start()
 
-    for load in loads[1:5]:
+    for load in loads[1:5] + loads[8:]:
         load.wait()
     kept = keep[...].astype(jnp.float32)
     scaled = width[...] * strands / (jnp.sum(kept, axis=1, keepdims=True) + 1.0)
@@ -153,11 +158,13 @@
     loads[5].wait()
     offset = here * tile
     ask_upper.wait()
-    outgoing[0] = pick_rows(columns(lists[0], lanes) - offset, guides, total)
+    ask_lower.wait()
+    wanted = jnp.concatenate([columns(lists[0], lanes), columns(lists[1], lanes)], axis=0)
+    both = pick_rows(wanted - offset, guides, total)
+    outgoing[0] = both[: blocks * listed]
+    outgoing[1] = both[blocks * listed :]
     to_lower = remote(outgoing.at[0], incoming.at[1], 4, lower)
     to_lower.start()
-    ask_lower.wait()
-    outgoing[1] = pick_rows(columns(lists[1], lanes) - offset, guides, total)
     to_upper = remote(outgoing.at[1], incoming.at[0], 5, upper)
     to_upper.start()
 
@@ -182,9 +189,9 @@
         return carry
 
     lax.fori_loop(0, screens * blocks, mixing, 0)
-    keep_tiles = pltpu.make_async_copy(tiles, tiles_hbm, local_sem.at[8])
+    keep_tiles = pltpu.make_async_copy(tiles, tiles_hbm, local_sem.at[9])
     keep_tiles.start()
-    keep_spreads = pltpu.make_async_copy(spreads, spreads_hbm, local_sem.at[9])
+    keep_spreads = pltpu.make_async_copy(spreads, spreads_hbm, local_sem.at[10])
     keep_spreads.start()
     loads[6].wait()
     loads[7].wait()
@@ -204,12 +211,12 @@
                 ]
 
     mapped(core)
-    keep_own = pltpu.make_async_copy(maps.at[core], maps_hbm.at[core], local_sem.at[10])
+    keep_own = pltpu.make_async_copy(maps.at[core], maps_hbm.at[core], local_sem.at[11])
     keep_own.start()
     give_rows.wait()
     mapped(1 - core)
     keep_other = pltpu.make_async_copy(
-        maps.at[1 - core], maps_hbm.at[1 - core], local_sem.at[11]
+        maps.at[1 - core], maps_hbm.at[1 - core], local_sem.at[12]
     )
     keep_other.start()
     keep_tiles.wait()
@@ -274,7 +281,6 @@
     count = blocks * listed
     fields = -(-(2 * joins + 2) // 8) * 8
     verts = tess_centre.shape[2]
-    vmem = pl.BlockSpec(memory_space=pltpu.VMEM)
     hbm = pl.BlockSpec(memory_space=pltpu.HBM)
     route = route.reshape(1, blocks)
     maps, spreads, tiles = pl.pallas_call(
@@ -284,7 +290,7 @@
             jax.ShapeDtypeStruct((screens * blocks, strands, 2 * listed), jnp.bfloat16),
             jax.ShapeDtypeStruct((screens, 1, blocks), jnp.int32),
         ),
-        in_specs=[hbm, hbm, hbm, vmem, hbm, hbm, hbm, hbm, hbm],
+        in_specs=[hbm, hbm, hbm, hbm, hbm, hbm, hbm, hbm, hbm],
         out_specs=(hbm, hbm, hbm),
         scratch_shapes=[
             pltpu.VMEM((screens, blocks, 2 * listed, verts), jnp.bfloat16),
@@ -293,6 +299,7 @@
             pltpu.VMEM(guides.shape, guides.dtype),
             pltpu.VMEM(neighbours.shape, jnp.int32),
             pltpu.VMEM(pick.shape, jnp.int32),
+            pltpu.VMEM(pick_weight.shape, pick_weight.dtype),
             pltpu.VMEM(keep.shape, jnp.int32),
             pltpu.VMEM(width.shape, jnp.float32),
             pltpu.VMEM(route.shape, jnp.int32),
@@ -303,8 +310,8 @@
             pltpu.VMEM((2, blocks, listed), jnp.int32),
             pltpu.VMEM((2, count, points), jnp.bfloat16),
             pltpu.VMEM((2, count, points), jnp.bfloat16),
-            pltpu.VMEM((count, points), jnp.float32),
-            pltpu.SemaphoreType.DMA((12,)),
+            pltpu.VMEM((2 * count, points), jnp.float32),
+            pltpu.SemaphoreType.DMA((13,)),
             pltpu.SemaphoreType.DMA((7,)),
             pltpu.SemaphoreType.DMA((7,)),
         ],

time: 24.3 us -> 24.2 us (level)
  no operation moved by 1% of the time
where the time goes in v4:
time: 24.2 us; the launch traced here: 24 us
  Pallas kernels  24 us (99%)
    pallas_call x1, Pallas kernels, shards(): pl.pallas_call(functools.partial(exchange, scalps), out_shape=(jax.ShapeD...  21 us
    pallas_call x1, Pallas kernels, shards(): pl.pallas_call(functools.partial(tessellate, cap), out_shape=jax.ShapeDty...  3.01 us

profile of v4, /device:TPU:0, one launch (start us, length us, event | category | flops | bytes accessed | tf_op | source)
XLA Modules:
  0.0 24.0 jit_solution(9500946842836599127)
XLA Ops:
  0.0 21.0 %shard_map.91 = (bf16[2,4,64,768]{3,2,1,0:T(8,128)(2,1)}, bf16[8,256,64]{2,1,0:T(8,128)(2,1)}, s32[2,1,4]{2,1,0:T(1,128)}) custom-call(bf16[4096,384]{1,0:T(8,128)(2,1)} %guides_hbm.1, s32[4,32]{1,0:T(4,128)} %near_hbm.1, s32[4,4,256]{2,1,0:T(4,128)} %pick_hbm.1, bf16[4,4,256]{2,1,0:T(4,128)(2,1)} %weight_hbm.1, s32[4,256]{1,0:T(4,128)} %keep_hbm.1, ...), custom_call_target="tpu_custom_call" | custom-call | tf_op jit(solution)/shard_map/pallas_call | solution.py:286
  21.0 3.0 %shard_map.92 = bf16[1536,768]{1,0:T(8,128)(2,1)} custom-call(s32[2,1,4]{2,1,0:T(1,128)} %get-tuple-element.8.tiles_hbm, bf16[2,4,64,768]{3,2,1,0:T(8,128)(2,1)} %get-tuple-element.9.maps_hbm, bf16[8,256,64]{2,1,0:T(8,128)(2,1)} %get-tuple-element.10.spreads_hbm), custom_call_target="tpu_custom_call" | custom-call | tf_op jit(solution)/shard_map/pallas_call | solution.py:322

commit v5 on v4

--- a/solution.py
+++ b/solution.py
@@ -159,16 +159,26 @@
     offset = here * tile
     ask_upper.wait()
     ask_lower.wait()
-    wanted = jnp.concatenate([columns(lists[0], lanes), columns(lists[1], lanes)], axis=0)
-    both = pick_rows(wanted - offset, guides, total)
-    outgoing[0] = both[: blocks * listed]
-    outgoing[1] = both[blocks * listed :]
-    to_lower = remote(outgoing.at[0], incoming.at[1], 4, lower)
-    to_lower.start()
-    to_upper = remote(outgoing.at[1], incoming.at[0], 5, upper)
-    to_upper.start()
-
-    rows[core] = pick_rows(columns(near[...], lanes) - offset, guides, total)
+    from_lower = columns(lists[0], lanes) - offset
+    from_upper = columns(lists[1], lanes) - offset
+    parts, part = rows.shape[1:3]
+    to_lower, to_upper = [], []
+    for h in range(parts):
+        span = slice(h * part, (h + 1) * part)
+        wanted = jnp.concatenate([from_lower[span], from_upper[span]], axis=0)
+        both = pick_rows(wanted, guides, total)
+        outgoing[0, h] = both[:part]
+        outgoing[1, h] = both[part:]
+        first = remote(outgoing.at[0, h], incoming.at[1, h], 4 + 2 * h, lower)
+        first.start()
+        to_lower.append(first)
+        second = remote(outgoing.at[1, h], incoming.at[0, h], 5 + 2 * h, upper)
+        second.start()
+        to_upper.append(second)
+
+    own = pick_rows(columns(near[...], lanes) - offset, guides, total)
+    for h in range(parts):
+        rows[core, h] = own[h * part : (h + 1) * part]
     give_data.wait()
     give_tiles.wait()
     names = lax.broadcasted_iota(jnp.int32, (listed, strands), 0).astype(jnp.float32)
@@ -195,34 +205,42 @@
     keep_spreads.start()
     loads[6].wait()
     loads[7].wait()
-    to_lower.wait()
-    to_upper.wait()
-    rows[core] = rows[core] + incoming[0] + incoming[1]
-    give_rows = remote(rows.at[core], rows.at[core], 6, pair)
-    give_rows.start()
-
-    def mapped(c):
+
+    group = blocks // parts
+    keeps = []
+
+    def mapped(c, h, at):
         for half, table in enumerate((centre, side)):
-            made = jnp.dot(rows[c], table[0], preferred_element_type=jnp.float32)
+            made = jnp.dot(rows[c, h], table[0], preferred_element_type=jnp.float32)
             made = made.astype(jnp.bfloat16)
-            for b in range(blocks):
-                maps[c, b, half * listed : (half + 1) * listed] = made[
+            for b in range(group):
+                maps[c, h * group + b, half * listed : (half + 1) * listed] = made[
                     b * listed : (b + 1) * listed
                 ]
-
-    mapped(core)
-    keep_own = pltpu.make_async_copy(maps.at[core], maps_hbm.at[core], local_sem.at[11])
-    keep_own.start()
-    give_rows.wait()
-    mapped(1 - core)
-    keep_other = pltpu.make_async_copy(
-        maps.at[1 - core], maps_hbm.at[1 - core], local_sem.at[12]
-    )
-    keep_other.start()
+        span = pl.ds(h * group, group)
+        copy = pltpu.make_async_copy(maps.at[c, span], maps_hbm.at[c, span], local_sem.at[at])
+        copy.start()
+        keeps.append(copy)
+
+    gives = []
+    for h in range(parts):
+        if h:
+            mapped(core, h - 1, 9 + 2 + h - 1)
+        to_lower[h].wait()
+        to_upper[h].wait()
+        rows[core, h] = rows[core, h] + incoming[0, h] + incoming[1, h]
+        give = remote(rows.at[core, h], rows.at[core, h], 4 + 2 * parts + h, pair)
+        give.start()
+        gives.append(give)
+    for h in range(parts):
+        if h == parts - 1:
+            mapped(core, h, 9 + 2 + h)
+        gives[h].wait()
+        mapped(1 - core, h, 9 + 2 + parts + h)
     keep_tiles.wait()
     keep_spreads.wait()
-    keep_own.wait()
-    keep_other.wait()
+    for copy in keeps:
+        copy.wait()
 
 
 def tessellate(
@@ -279,6 +297,8 @@
     joins = pick.shape[1]
     cap = blocks // screens + blocks // 4
     count = blocks * listed
+    parts = 2 if blocks % 2 == 0 else 1
+    part = count // parts
     fields = -(-(2 * joins + 2) // 8) * 8
     verts = tess_centre.shape[2]
     hbm = pl.BlockSpec(memory_space=pltpu.HBM)
@@ -305,15 +325,15 @@
             pltpu.VMEM(route.shape, jnp.int32),
             pltpu.VMEM(tess_centre.shape, jnp.bfloat16),
             pltpu.VMEM(tess_side.shape, jnp.bfloat16),
-            pltpu.VMEM((screens, count, points), jnp.bfloat16),
+            pltpu.VMEM((screens, parts, part, points), jnp.bfloat16),
             pltpu.VMEM((screens, blocks, fields, strands), jnp.float32),
             pltpu.VMEM((2, blocks, listed), jnp.int32),
-            pltpu.VMEM((2, count, points), jnp.bfloat16),
-            pltpu.VMEM((2, count, points), jnp.bfloat16),
+            pltpu.VMEM((2, parts, part, points), jnp.bfloat16),
+            pltpu.VMEM((2, parts, part, points), jnp.bfloat16),
             pltpu.VMEM((2 * count, points), jnp.float32),
-            pltpu.SemaphoreType.DMA((13,)),
-            pltpu.SemaphoreType.DMA((7,)),
-            pltpu.SemaphoreType.DMA((7,)),
+            pltpu.SemaphoreType.DMA((11 + 2 * parts,)),
+            pltpu.SemaphoreType.DMA((4 + 3 * parts,)),
+            pltpu.SemaphoreType.DMA((4 + 3 * parts,)),
         ],
         compiler_params=pltpu.CompilerParams(
             collective_id=0, has_side_effects=True, vmem_limit_bytes=56 * 1024 * 1024

time: 24.2 us -> 24.3 us (level)
  no operation moved by 1% of the time
where the time goes in v5:
time: 24.3 us; the launch traced here: 24.1 us
  Pallas kernels  24.1 us (99%)
    pallas_call x1, Pallas kernels, shards(): pl.pallas_call(functools.partial(exchange, scalps), out_shape=(jax.ShapeD...  21.1 us
    pallas_call x1, Pallas kernels, shards(): pl.pallas_call(functools.partial(tessellate, cap), out_shape=jax.ShapeDty...  3.01 us

profile of v5, /device:TPU:0, one launch (start us, length us, event | category | flops | bytes accessed | tf_op | source)
XLA Modules:
  0.0 24.1 jit_solution(1018971267106514337)
XLA Ops:
  0.0 21.1 %shard_map.91 = (bf16[2,4,64,768]{3,2,1,0:T(8,128)(2,1)}, bf16[8,256,64]{2,1,0:T(8,128)(2,1)}, s32[2,1,4]{2,1,0:T(1,128)}) custom-call(bf16[4096,384]{1,0:T(8,128)(2,1)} %guides_hbm.1, s32[4,32]{1,0:T(4,128)} %near_hbm.1, s32[4,4,256]{2,1,0:T(4,128)} %pick_hbm.1, bf16[4,4,256]{2,1,0:T(4,128)(2,1)} %weight_hbm.1, s32[4,256]{1,0:T(4,128)} %keep_hbm.1, ...), custom_call_target="tpu_custom_call" | custom-call | tf_op jit(solution)/shard_map/pallas_call | solution.py:306
  21.1 3.0 %shard_map.92 = bf16[1536,768]{1,0:T(8,128)(2,1)} custom-call(s32[2,1,4]{2,1,0:T(1,128)} %get-tuple-element.8.tiles_hbm, bf16[2,4,64,768]{3,2,1,0:T(8,128)(2,1)} %get-tuple-element.9.maps_hbm, bf16[8,256,64]{2,1,0:T(8,128)(2,1)} %get-tuple-element.10.spreads_hbm), custom_call_target="tpu_custom_call" | custom-call | tf_op jit(solution)/shard_map/pallas_call | solution.py:342

commit v6 on v2

--- a/solution.py
+++ b/solution.py
@@ -24,14 +24,17 @@
     tile = guides.shape[0]
     chunk = min(CHUNK, tile)
     lane = lax.broadcasted_iota(jnp.int32, (rows, lanes), 1)
+    high = wanted >> (lanes.bit_length() - 1)
+    low = jnp.where((wanted & (lanes - 1)) == lane, 1.0, 0.0).astype(jnp.bfloat16)
     total[:rows] = jnp.zeros((rows, guides.shape[1]), jnp.float32)
 
     def body(i, carry):
         base = pl.multiple_of(i * chunk, chunk)
+        group = (high - i * (chunk // lanes)).astype(jnp.float32).astype(jnp.bfloat16)
         hit = jnp.concatenate(
             [
-                jnp.where(wanted == lane + (base + at), 1.0, 0.0).astype(jnp.bfloat16)
-                for at in range(0, chunk, lanes)
+                jnp.where(group == jnp.bfloat16(at), low, jnp.bfloat16(0))
+                for at in range(chunk // lanes)
             ],
             axis=1,
         )
@@ -46,21 +49,27 @@
 
 def exchange(
     scalps,
+    cap,
     guides_hbm,
     near_hbm,
     pick_hbm,
-    weight,
+    weight_hbm,
     keep_hbm,
     width_hbm,
     route_hbm,
     centre_hbm,
     side_hbm,
+    out,
+    tiles_smem,
+    held,
+    out_sems,
     maps,
     spreads,
     tiles,
     guides,
     near,
     pick,
+    weight,
     keep,
     width,
     route,
@@ -102,6 +111,7 @@
                 (guides_hbm, guides),
                 (centre_hbm, centre),
                 (side_hbm, side),
+                (weight_hbm, weight),
             )
         )
     ]
@@ -125,7 +135,7 @@
     ask_upper.start()
     ask_lower.start()
 
-    for load in loads[1:5]:
+    for load in loads[1:5] + loads[8:]:
         load.wait()
     kept = keep[...].astype(jnp.float32)
     scaled = width[...] * strands / (jnp.sum(kept, axis=1, keepdims=True) + 1.0)
@@ -150,11 +160,13 @@
     loads[5].wait()
     offset = here * tile
     ask_upper.wait()
-    outgoing[0] = pick_rows(columns(lists[0], lanes) - offset, guides, total)
+    ask_lower.wait()
+    wanted = jnp.concatenate([columns(lists[0], lanes), columns(lists[1], lanes)], axis=0)
+    both = pick_rows(wanted - offset, guides, total)
+    outgoing[0] = both[: blocks * listed]
+    outgoing[1] = both[blocks * listed :]
     to_lower = remote(outgoing.at[0], incoming.at[1], 4, lower)
     to_lower.start()
-    ask_lower.wait()
-    outgoing[1] = pick_rows(columns(lists[1], lanes) - offset, guides, total)
     to_upper = remote(outgoing.at[1], incoming.at[0], 5, upper)
     to_upper.start()
 
@@ -179,6 +191,9 @@
         return carry
 
     lax.fori_loop(0, screens * blocks, mixing, 0)
+    read_tiles = pltpu.make_async_copy(tiles, tiles_smem, local_sem.at[9])
+    read_tiles.start()
+    read_tiles.wait()
     loads[6].wait()
     loads[7].wait()
     to_lower.wait()
@@ -196,23 +211,17 @@
                     b * listed : (b + 1) * listed
                 ]
 
-    mapped(core)
-    give_rows.wait()
-    mapped(1 - core)
-
-
-def tessellate(cap, tiles, maps, spreads, out, held, sems):
-    screens, blocks = maps.shape[:2]
-    strands = spreads.shape[1]
-    mine = lax.axis_index("screen")
     copies = []
-    for source in range(screens):
+    for turn, source in enumerate((core, 1 - core)):
+        if turn:
+            give_rows.wait()
+        mapped(source)
         for place in range(cap):
             rank = jnp.int32(0)
             block = jnp.int32(0)
             found = jnp.int32(0)
             for b in range(blocks):
-                same = (tiles[source, 0, b] == mine).astype(jnp.int32)
+                same = (tiles_smem[source, 0, b] == core).astype(jnp.int32)
                 hit = same * (rank == place).astype(jnp.int32)
                 block = block + hit * b
                 found = found + hit
@@ -225,7 +234,9 @@
                 spread, maps[source, block], preferred_element_type=jnp.float32
             ).astype(out.dtype)
             copy = pltpu.make_async_copy(
-                held.at[slot], out.at[pl.ds(slot * strands, strands)], sems.at[slot]
+                held.at[slot],
+                out.at[pl.ds(pl.multiple_of(slot * strands, strands), strands)],
+                out_sems.at[turn * cap + place],
             )
             copy.start()
             copies.append(copy)
@@ -244,22 +255,24 @@
     count = blocks * listed
     fields = -(-(2 * joins + 2) // 8) * 8
     verts = tess_centre.shape[2]
-    vmem = pl.BlockSpec(memory_space=pltpu.VMEM)
     hbm = pl.BlockSpec(memory_space=pltpu.HBM)
     route = route.reshape(1, blocks)
-    maps, spreads, tiles = pl.pallas_call(
-        functools.partial(exchange, scalps),
-        out_shape=(
-            jax.ShapeDtypeStruct((screens, blocks, 2 * listed, verts), jnp.bfloat16),
-            jax.ShapeDtypeStruct((screens * blocks, strands, 2 * listed), jnp.bfloat16),
-            jax.ShapeDtypeStruct((screens, 1, blocks), jnp.int32),
-        ),
-        in_specs=[hbm, hbm, hbm, vmem, hbm, hbm, hbm, hbm, hbm],
-        out_specs=(vmem, vmem, vmem),
+    return pl.pallas_call(
+        functools.partial(exchange, scalps, cap),
+        out_shape=jax.ShapeDtypeStruct((screens * cap * strands, verts), jnp.bfloat16),
+        in_specs=[hbm, hbm, hbm, hbm, hbm, hbm, hbm, hbm, hbm],
+        out_specs=hbm,
         scratch_shapes=[
+            pltpu.SMEM((screens, 1, blocks), jnp.int32),
+            pltpu.VMEM((screens * cap, strands, verts), jnp.bfloat16),
+            pltpu.SemaphoreType.DMA((screens * cap,)),
+            pltpu.VMEM((screens, blocks, 2 * listed, verts), jnp.bfloat16),
+            pltpu.VMEM((screens * blocks, strands, 2 * listed), jnp.bfloat16),
+            pltpu.VMEM((screens, 1, blocks), jnp.int32),
             pltpu.VMEM(guides.shape, guides.dtype),
             pltpu.VMEM(neighbours.shape, jnp.int32),
             pltpu.VMEM(pick.shape, jnp.int32),
+            pltpu.VMEM(pick_weight.shape, pick_weight.dtype),
             pltpu.VMEM(keep.shape, jnp.int32),
             pltpu.VMEM(width.shape, jnp.float32),
             pltpu.VMEM(route.shape, jnp.int32),
@@ -270,26 +283,15 @@
             pltpu.VMEM((2, blocks, listed), jnp.int32),
             pltpu.VMEM((2, count, points), jnp.bfloat16),
             pltpu.VMEM((2, count, points), jnp.bfloat16),
-            pltpu.VMEM((count, points), jnp.float32),
-            pltpu.SemaphoreType.DMA((8,)),
+            pltpu.VMEM((2 * count, points), jnp.float32),
+            pltpu.SemaphoreType.DMA((10,)),
             pltpu.SemaphoreType.DMA((7,)),
             pltpu.SemaphoreType.DMA((7,)),
         ],
         compiler_params=pltpu.CompilerParams(
-            collective_id=0, has_side_effects=True, vmem_limit_bytes=24 * 1024 * 1024
+            collective_id=0, has_side_effects=True, vmem_limit_bytes=56 * 1024 * 1024
         ),
     )(guides, neighbours, pick, pick_weight, keep, width, route, tess_centre, tess_side)
-    return pl.pallas_call(
-        functools.partial(tessellate, cap),
-        out_shape=jax.ShapeDtypeStruct((screens * cap * strands, verts), jnp.bfloat16),
-        in_specs=[pl.BlockSpec(memory_space=pltpu.SMEM), vmem, vmem],
-        out_specs=hbm,
-        scratch_shapes=[
-            pltpu.VMEM((screens * cap, strands, verts), jnp.bfloat16),
-            pltpu.SemaphoreType.DMA((screens * cap,)),
-        ],
-        compiler_params=pltpu.CompilerParams(vmem_limit_bytes=24 * 1024 * 1024),
-    )(tiles, maps, spreads)
 
 
 def solution(mesh):

time: 30.4 us -> 25 us (0.82)
  local copies, waits for them, and re-layouts: 8.14 us -> 3.22 us
    unnamed x18 -> x1, local copies, waits for them, and re-layouts: 8.14 us -> 3.22 us
    pallas_call x2 -> x1, Pallas kernels: 21.9 us -> 21.6 us  [shards(): pl.pallas_call(functools.partial(exchange, scalps, cap), out_shape=jax.Sh...]
where the time goes in v6:
time: 25 us; the launch traced here: 24.8 us
  Pallas kernels  21.6 us (86%)
  local copies, waits for them, and re-layouts  3.22 us (13%)
    pallas_call x1, Pallas kernels, shards(): pl.pallas_call(functools.partial(exchange, scalps, cap), out_shape=jax.Sh...  21.6 us
    unnamed x1, local copies, waits for them, and re-layouts  3.22 us

profile of v6, /device:TPU:0, one launch (start us, length us, event | category | flops | bytes accessed | tf_op | source)
XLA Modules:
  0.0 24.8 jit_solution(14352725154610932400)
XLA Ops:
  0.0 21.6 %shard_map.91 = bf16[1536,768]{1,0:T(8,128)(2,1)} custom-call(bf16[4096,384]{1,0:T(8,128)(2,1)} %guides_hbm.1, s32[4,32]{1,0:T(4,128)} %near_hbm.1, s32[4,4,256]{2,1,0:T(4,128)} %pick_hbm.1, bf16[4,4,256]{2,1,0:T(4,128)(2,1)} %weight_hbm.1, s32[4,256]{1,0:T(4,128)} %keep_hbm.1, f32[4,256]{1,0:T(4,128)} %width_hbm.1, s32[1,4]{1,0:T(1,128)} %bitcast.1, ...), custom_call_target="tpu_custom_call" | custom-call | tf_op jit(solution)/shard_map/pallas_call | solution.py:260
  21.6 3.2 %copy.11 = bf16[1536,768]{1,0:T(8,128)(2,1)} copy(bf16[1536,768]{1,0:T(8,128)(2,1)} %shard_map.91) | data formatting | bytes 4718592
